TPU v7x, 32 devices: a whole 2x2x4 slice. The times are simulated.
32 devices in a mesh: parts: 1, ep: 32 (over z, y, x, core), ex: 1.
Axes of the slice: x: 2, y: 2, z: 4, core: 2. Of those that a mesh axis runs over, the one named last changes fastest.
Arguments:
- residual: bfloat16 [256, 4096], P(('parts', 'ep', 'ex')), may hold values from -6 to 6
- queries: bfloat16 [256, 4096], P(('parts', 'ep', 'ex')), may hold values from -80 to 80
- new_kv: bfloat16 [256, 512], P(('parts', 'ep', 'ex')), may hold values from -4 to 4
- cache_pool: bfloat16 [2048, 16, 512], P(('parts', 'ep', 'ex')), may hold values from -6 to 6
- page_table: int32 [32, 64], P(('parts', 'ep', 'ex')), may hold values from 0 to 63, each once within a row
- context_len: int32 [32, 8], P(('parts', 'ep', 'ex')), may hold values from 1 to 128, 576 in all within a row
- prefill_hidden: bfloat16 [1792, 4096], P(('parts', 'ep', 'ex')), may hold values from -6 to 6
- prefill_kv: bfloat16 [1792, 512], P(('parts', 'ep', 'ex')), may hold values from -6 to 6
- prefill_dest: int32 [1792, 1], P(('parts', 'ep', 'ex')), may hold values from 0 to 31; in each aligned block of 56 rows (0 to 55, 56 to 111, ...) at most 3 rows name the same one
- prefill_slot: int32 [1792], P(('parts', 'ep', 'ex')), may hold values from 0 to 7
- expert_ids: int32 [2048, 8], P(('parts', 'ep', 'ex')), may hold values from 0 to 31, all different within a row; in each aligned block of 64 rows (0 to 63, 64 to 127, ...) at most 20 rows name the same one
- gate_values: float32 [2048, 8], P(('parts', 'ep', 'ex')), may hold values from 0.05 to 0.3
- norm_gain: float32 [4096], replicated, may hold values from 0.5 to 1.5
- gate_weight: bfloat16 [32, 4096, 768], P('ep', None, 'ex'), may hold values from -0.09375 to 0.09375
- up_weight: bfloat16 [32, 4096, 768], P('ep', None, 'ex'), may hold values from -0.09375 to 0.09375
- down_weight: bfloat16 [32, 768, 4096], P('ep', 'ex'), may hold values from -0.21875 to 0.21875
Outputs:
- decode_out: bfloat16 [256, 4096], P(('parts', 'ep', 'ex'))
- prefill_out: bfloat16 [1792, 4096], P(('parts', 'ep', 'ex'))
Inputs may be any that keep to these rules, and one draw needn't show every extreme that they name: `page_table`: each row is a permutation of one device's 64 local pages; request i of that device reads entries i * 8 to (i + 1) * 8 - 1 in order. `context_len`: each device's lengths sum to 576 and one of them is 128. `prefill_dest`: device index in ep+ex order inside the group; at most 3 of one device's prefill tokens name one device, and that many do on some device. `expert_ids`: the experts of a row differ; at most 20 of one device's 64 rows name one expert, and that many do on some device.
All inputs are finite; a program needn't handle non-finite values.
Results may differ from a plain program's by a relative error of at most 0.007.
Values may be sent and summed in bfloat16 or wider, within the bound.
A program may use at most 128 MiB of HBM per device.

v0:
```python
import jax
import jax.numpy as jnp
from jax import lax
from jax.sharding import PartitionSpec as P

HD = 128
KVH = 2


neg_big = -1e30
eps = 1e-06


def attend(queries, new_kv, cache, context_len, hand_kv, hand_ok):
    row_count = queries.shape[0]
    kv_width = new_kv.shape[1] // 2
    group_size = queries.shape[1] // kv_width
    positions = cache.shape[1]
    query_heads = queries.reshape(row_count, KVH, group_size, HD)
    cache_keys = cache[:, :, :kv_width].reshape(row_count, positions, KVH, HD)
    cache_values = cache[:, :, kv_width:].reshape(row_count, positions, KVH, HD)
    hand_keys = hand_kv[:, :kv_width].reshape(-1, KVH, HD)
    hand_values = hand_kv[:, kv_width:].reshape(-1, KVH, HD)
    own_keys = new_kv[:, :kv_width].reshape(row_count, KVH, HD)
    own_values = new_kv[:, kv_width:].reshape(row_count, KVH, HD)
    score_scale = HD ** (-0.5)
    cache_scores = (
        jnp.einsum("rgjd,rtgd->rgjt", query_heads, cache_keys, preferred_element_type=jnp.float32)
        * score_scale
    )
    live_mask = jnp.arange(positions, dtype=jnp.int32)[None, :] < context_len[:, None]
    cache_scores = jnp.where(live_mask[:, None, None, :], cache_scores, neg_big)
    hand_scores = (
        jnp.einsum("rgjd,mgd->rgjm", query_heads, hand_keys, preferred_element_type=jnp.float32)
        * score_scale
    )
    hand_scores = jnp.where(hand_ok[:, None, None, :], hand_scores, neg_big)
    own_scores = (
        jnp.einsum("rgjd,rgd->rgj", query_heads, own_keys, preferred_element_type=jnp.float32)
        * score_scale
    )
    largest = jnp.maximum(
        jnp.maximum(jnp.max(cache_scores, -1), jnp.max(hand_scores, -1)), own_scores
    )
    cache_exp = jnp.exp(cache_scores - largest[..., None])
    hand_exp = jnp.exp(hand_scores - largest[..., None])
    own_exp = jnp.exp(own_scores - largest)
    denominator = jnp.sum(cache_exp, -1) + jnp.sum(hand_exp, -1) + own_exp
    cache_probs = (cache_exp / denominator[..., None]).astype(jnp.bfloat16)
    hand_probs = (hand_exp / denominator[..., None]).astype(jnp.bfloat16)
    own_probs = (own_exp / denominator).astype(jnp.bfloat16)
    attended = jnp.einsum(
        "rgjt,rtgd->rgjd", cache_probs, cache_values, preferred_element_type=jnp.float32
    )
    attended = attended + jnp.einsum(
        "rgjm,mgd->rgjd", hand_probs, hand_values, preferred_element_type=jnp.float32
    )
    attended = (
        attended
        + own_probs.astype(jnp.float32)[..., None] * own_values.astype(jnp.float32)[:, :, None, :]
    )
    return attended.reshape(row_count, -1)


def expert_terms(slot_rows, gate_weight, up_weight, down_weight):
    gate_act = jnp.dot(slot_rows, gate_weight[0], preferred_element_type=jnp.float32)
    up_act = jnp.dot(slot_rows, up_weight[0], preferred_element_type=jnp.float32)
    hidden = (jax.nn.silu(gate_act) * up_act).astype(jnp.bfloat16)
    return jnp.dot(hidden, down_weight[0], preferred_element_type=jnp.float32)


def on_device(
    residual,
    queries,
    new_kv,
    cache_pool,
    page_table,
    context_len,
    prefill_hidden,
    prefill_kv,
    prefill_dest,
    prefill_slot,
    expert_ids,
    gate_values,
    norm_gain,
    gate_weight,
    up_weight,
    down_weight,
):
    decode_rows = residual.shape[0]
    model_width = residual.shape[1]
    devices = lax.axis_size(("ep", "ex"))
    pre_rows = prefill_kv.shape[0]
    pages = page_table.reshape(decode_rows, -1)
    cache = cache_pool[pages].reshape(decode_rows, -1, cache_pool.shape[2])
    lengths = context_len.reshape(decode_rows)
    kv_slots = max(1, (5 * pre_rows + 4 * devices - 1) // (4 * devices))
    target = prefill_dest[:, 0]
    target_hot = (target[:, None] == jnp.arange(devices, dtype=jnp.int32)[None, :]).astype(
        jnp.int32
    )
    target_rank = jnp.sum(jnp.cumsum(target_hot, axis=0) * target_hot, axis=1) - 1
    target_place = target * kv_slots + target_rank
    send_kv = (
        jnp.zeros((devices * kv_slots, prefill_kv.shape[1]), jnp.bfloat16)
        .at[target_place]
        .set(prefill_kv)
    )
    send_slot = jnp.full((devices * kv_slots,), -1, jnp.int32).at[target_place].set(prefill_slot)
    hand_kv, hand_slot = (
        lax.all_to_all(send_kv, ("ep", "ex"), split_axis=0, concat_axis=0, tiled=True),
        lax.all_to_all(send_slot, ("ep", "ex"), split_axis=0, concat_axis=0, tiled=True),
    )
    hand_ok = hand_slot[None, :] == jnp.arange(decode_rows, dtype=jnp.int32)[:, None]
    attention = attend(queries, new_kv, cache, lengths, hand_kv, hand_ok)
    residual_sum = jnp.concatenate(
        [residual.astype(jnp.float32) + attention, prefill_hidden.astype(jnp.float32)], axis=0
    )
    mean_square = jnp.mean(residual_sum * residual_sum, axis=1, keepdims=True)
    normed = (residual_sum * lax.rsqrt(mean_square + eps) * norm_gain).astype(jnp.bfloat16)
    row_total = normed.shape[0]
    top_count = expert_ids.shape[1]
    experts = lax.axis_size("ep")
    capacity = min(
        row_total, max(2, (5 * row_total * top_count + 4 * experts - 1) // (4 * experts))
    )
    chosen = expert_ids.reshape(-1)
    chosen_hot = (chosen[:, None] == jnp.arange(experts, dtype=jnp.int32)[None, :]).astype(
        jnp.int32
    )
    chosen_rank = jnp.sum(jnp.cumsum(chosen_hot, axis=0) * chosen_hot, axis=1) - 1
    slot_place = chosen * capacity + chosen_rank
    source_row = jnp.arange(row_total * top_count, dtype=jnp.int32) // top_count
    slot_source = jnp.zeros((experts * capacity,), jnp.int32).at[slot_place].set(source_row)
    slot_used = jnp.zeros((experts * capacity,), jnp.bool_).at[slot_place].set(True)
    outgoing = jnp.where(slot_used[:, None], normed[slot_source], jnp.zeros((), jnp.bfloat16))
    arrived = lax.all_to_all(outgoing, "ep", split_axis=0, concat_axis=0, tiled=True)
    partial_out = expert_terms(
        lax.all_gather(arrived, "ex", axis=0, tiled=True), gate_weight, up_weight, down_weight
    )
    summed = lax.psum_scatter(
        partial_out.astype(jnp.bfloat16), "ex", scatter_dimension=0, tiled=True
    )
    returned = lax.all_to_all(summed, "ep", split_axis=0, concat_axis=0, tiled=True)
    picked = returned[slot_place].reshape(row_total, top_count, model_width)
    mixture = jnp.einsum("rk,rkd->rd", gate_values, picked.astype(jnp.float32))
    result = (residual_sum + mixture).astype(jnp.bfloat16)
    return (result[:decode_rows], result[decode_rows:])


def solution(mesh):
    in_specs = (
        P(("parts", "ep", "ex"), None),
        P(("parts", "ep", "ex"), None),
        P(("parts", "ep", "ex"), None),
        P(("parts", "ep", "ex"), None, None),
        P(("parts", "ep", "ex"), None),
        P(("parts", "ep", "ex"), None),
        P(("parts", "ep", "ex"), None),
        P(("parts", "ep", "ex"), None),
        P(("parts", "ep", "ex"), None),
        P(("parts", "ep", "ex")),
        P(("parts", "ep", "ex"), None),
        P(("parts", "ep", "ex"), None),
        P(),
        P("ep", None, "ex"),
        P("ep", None, "ex"),
        P("ep", "ex", None),
    )
    out_specs = (P(("parts", "ep", "ex"), None), P(("parts", "ep", "ex"), None))
    return jax.shard_map(
        on_device, mesh=mesh, in_specs=in_specs, out_specs=out_specs, check_vma=False
    )
```

profile of v0, /device:TPU:8, one launch (start us, length us, event | category | flops | bytes accessed | tf_op | source)
XLA Modules:
  0.0 403.2 jit_solution(9887596448626397577)
XLA Ops:
  0.7 0.8 fusion.31
  1.5 0.1 reduce_window_sum.26
  1.6 0.8 select_reduce_fusion
  2.5 0.7 fusion.43
  3.1 0.9 scatter_custom_fusion
  4.0 0.7 all_to_all.28
  4.7 6.0 %all-to-all-start = ((s32[32,3,1]{1,2,0:T(1,128)}), s32[32,3,1]{1,2,0:T(1,128)S(1)}, u32[]{:S(2)}, u32[]{:S(2)}) async-start(s32[32,3,1]{1,2,0:T(1,128)} %bitcast.8), calls=%async_computation | async-start | bytes 32768 | tf_op jit(solution)/shard_map/all_to_all | solution.py:112
  10.8 0.8 copy.108
  11.5 0.1 eq.71
  11.6 0.1 eq.67
  11.7 0.7 broadcast_multiply_fusion
  12.4 0.6 broadcast.193
  13.0 1.4 reduce.9
  14.4 0.1 reshape.198
  14.5 0.1 reshape.212
  14.6 0.6 gather_fusion
  15.2 0.1 fusion.47
  15.3 0.3 copy.91
  15.6 0.1 iota_compare_fusion.4
  15.7 1.2 reduce-window.6
  16.9 0.2 slice_reduce_fusion
  17.1 0.1 fusion.18
  17.3 0.1 copy.107
  17.3 0.1 mul.105
  17.4 2.4 scatter_custom_fusion.3
  19.9 0.1 fusion.24
  20.1 0.3 fusion.49
  20.4 1.1 scatter_custom_fusion.1
  21.5 0.7 all_to_all.30
  22.3 0.3 copy.101
  22.6 0.1 convert_element_type.57
  22.6 2.4 scatter_custom_fusion.2
  25.1 0.1 broadcast_in_dim.83
  25.2 5.8 %all-to-all-start.1 = ((bf16[32,3,512]{2,1,0:T(4,128)(2,1)}), bf16[32,3,512]{2,1,0:T(4,128)(2,1)S(1)}, u32[]{:S(2)}, u32[]{:S(2)}) async-start(bf16[32,3,512]{2,1,0:T(4,128)(2,1)} %all_to_all.30), calls=%async_computation.1 | async-start | bytes 262144 | tf_op jit(solution)/shard_map/all_to_all | solution.py:111
  31.1 0.7 reduce.8
  31.8 0.1 eq.63
  31.9 6.3 %all-to-all-done.1 = bf16[32,3,512]{2,1,0:T(4,128)(2,1)S(1)} async-done(((bf16[32,3,512]{2,1,0:T(4,128)(2,1)}), bf16[32,3,512]{2,1,0:T(4,128)(2,1)S(1)}, u32[]{:S(2)}, u32[]{:S(2)}) %all-to-all-start.1) | async-done | bytes 98336 | tf_op jit(solution)/shard_map/all_to_all | solution.py:111
  38.2 0.1 all_to_all.32
  38.3 0.3 fusion.48
  38.6 0.2 fusion.16
  38.8 0.2 fusion.15
  39.1 0.3 convolution_bitcast_fusion
  39.3 0.4 fusion.11
  39.7 0.1 bitcast_add_fusion.1
  39.8 0.2 multiply_reduce_fusion
  40.0 0.2 multiply_convert_fusion.1
  40.2 5.4 %gather_fusion.1 = bf16[640,4096]{1,0:T(8,128)(2,1)} fusion(bf16[64,4096]{1,0:T(8,128)(2,1)S(1)} %multiply_convert_fusion.1, s32[1024]{0:T(1024)S(1)} %pad_clamp_fusion.1), kind=kCustom, calls=%fused_computation.1 | custom fusion | bytes 10488320 | tf_op jit(solution)/shard_map/gather | solution.py:136
  45.6 7.7 %gather.13 = bf16[32,20,4096]{2,1,0:T(8,128)(2,1)} reshape(bf16[640,4096]{1,0:T(8,128)(2,1)} %gather_fusion.1) | data formatting | bytes 10485760 | tf_op jit(solution)/shard_map/gather | solution.py:136
  53.3 3.3 broadcast_select_fusion
  56.5 141.2 %all_to_all.42 = bf16[32,20,4096]{2,1,0:T(8,128)(2,1)} all-to-all(bf16[32,20,4096]{2,1,0:T(8,128)(2,1)S(1)} %broadcast_select_fusion), channel_id=1, replica_groups=mesh['parts'=1,'ep'=32,'ex'=1] {'ep'}, dimensions={0} | all-to-all | bytes 10485760 | tf_op jit(solution)/shard_map/all_to_all | solution.py:137
  197.7 7.8 %all_to_all.34 = bf16[640,4096]{1,0:T(8,128)(2,1)} reshape(bf16[32,20,4096]{2,1,0:T(8,128)(2,1)} %all_to_all.42) | data formatting | bytes 10485760 | tf_op jit(solution)/shard_map/all_to_all | solution.py:137
  205.6 8.1 %fusion.3 = f32[640,768]{1,0:T(8,128)S(1)} fusion(bf16[640,4096]{1,0:T(8,128)(2,1)} %all_to_all.34, bf16[1,4096,768]{2,1,0:T(8,128)(2,1)} %param.29), kind=kOutput, calls=%fused_computation.11 | convolution fusion | flops 4026531840 | bytes 13500416 | tf_op jit(solution)/shard_map/dot_general | solution.py:66
  213.7 7.2 %multiply_convert_fusion = bf16[640,768]{1,0:T(8,128)(2,1)S(1)} fusion(f32[640,768]{1,0:T(8,128)S(1)} %fusion.3, bf16[640,4096]{1,0:T(8,128)(2,1)S(1)} %copy-done.2, bf16[1,4096,768]{2,1,0:T(8,128)(2,1)} %param.30), kind=kOutput, calls=%fused_computation.16 | convolution fusion | flops 4029480960 | bytes 14483456 | tf_op jit(solution)/shard_map/dot_general | solution.py:67
  220.9 8.8 %convolution_convert_fusion = bf16[640,4096]{1,0:T(8,128)(2,1)} fusion(bf16[640,768]{1,0:T(8,128)(2,1)S(1)} %multiply_convert_fusion, bf16[1,768,4096]{2,1,0:T(8,128)(2,1)} %param.31), kind=kOutput, calls=%fused_computation.7 | convolution fusion | flops 4029153280 | bytes 12517376 | tf_op jit(solution)/shard_map/dot_general | solution.py:69
  229.6 7.6 %all_to_all.35 = bf16[32,20,4096]{2,1,0:T(8,128)(2,1)} reshape(bf16[640,4096]{1,0:T(8,128)(2,1)} %convolution_convert_fusion) | data formatting | bytes 10485760 | tf_op jit(solution)/shard_map/all_to_all | solution.py:144
  237.2 4.7 %all-to-all-start.3 = ((bf16[32,20,4096]{2,1,0:T(8,128)(2,1)}), bf16[32,20,4096]{2,1,0:T(8,128)(2,1)}, u32[]{:S(2)}, u32[]{:S(2)}) async-start(bf16[32,20,4096]{2,1,0:T(8,128)(2,1)} %all_to_all.35), calls=%async_computation.3 | async-start | bytes 12582912 | tf_op jit(solution)/shard_map/all_to_all | solution.py:144
  242.0 0.1 copy.116
  242.1 135.9 %all-to-all-done.3 = bf16[32,20,4096]{2,1,0:T(8,128)(2,1)} async-done(((bf16[32,20,4096]{2,1,0:T(8,128)(2,1)}), bf16[32,20,4096]{2,1,0:T(8,128)(2,1)}, u32[]{:S(2)}, u32[]{:S(2)}) %all-to-all-start.3) | async-done | bytes 5242912 | tf_op jit(solution)/shard_map/all_to_all | solution.py:144
  378.0 7.8 %all_to_all.37 = bf16[640,4096]{1,0:T(8,128)(2,1)} reshape(bf16[32,20,4096]{2,1,0:T(8,128)(2,1)} %all-to-all-done.3) | data formatting | bytes 10485760 | tf_op jit(solution)/shard_map/all_to_all | solution.py:144
  385.9 11.8 %gather_fusion.2 = bf16[512,4096]{1,0:T(8,128)(2,1)} fusion(bf16[640,4096]{1,0:T(8,128)(2,1)} %all_to_all.37, s32[1024]{0:T(1024)S(1)} %pad_clamp_fusion), kind=kCustom, calls=%fused_computation.2 | custom fusion | bytes 8390656 | tf_op jit(solution)/shard_map/gather | solution.py:145
  397.7 3.4 fusion.5
  401.1 0.7 fusion.14
  401.8 0.8 slice.52
  402.6 0.6 slice.51
  (44 shorter events, 0.2 us)
Async XLA Ops:
  0.6 13.9 %copy-start = (bf16[64,16,512]{2,1,0:T(8,128)(2,1)S(1)}, bf16[64,16,512]{2,1,0:T(8,128)(2,1)}, u32[]{:S(2)}) copy-start(bf16[64,16,512]{2,1,0:T(8,128)(2,1)} %param.19) | copy-start | bytes 3145732
  0.6 15.0 %copy-start.9 = (s32[1,8]{1,0:T(1,128)S(1)}, s32[1,8]{1,0:T(1,128)}, u32[]{:S(2)}) copy-start(s32[1,8]{1,0:T(1,128)} %param.21) | copy-start | bytes 100
  0.7 15.0 %copy-start.7 = (bf16[8,512]{1,0:T(8,128)(2,1)S(1)}, bf16[8,512]{1,0:T(8,128)(2,1)}, u32[]{:S(2)}) copy-start(bf16[8,512]{1,0:T(8,128)(2,1)} %param.18) | copy-start | bytes 24580
  0.7 19.3 %copy-start.4 = (bf16[8,4096]{1,0:T(8,128)(2,1)S(1)}, bf16[8,4096]{1,0:T(8,128)(2,1)}, u32[]{:S(2)}) copy-start(bf16[8,4096]{1,0:T(8,128)(2,1)} %param.17) | copy-start | bytes 196612
  0.7 21.9 %copy-start.3 = (bf16[56,4096]{1,0:T(8,128)(2,1)S(1)}, bf16[56,4096]{1,0:T(8,128)(2,1)}, u32[]{:S(2)}) copy-start(bf16[56,4096]{1,0:T(8,128)(2,1)} %param.22) | copy-start | bytes 1376260
  4.7 20.5 %all-to-all-start = ((s32[32,3,1]{1,2,0:T(1,128)}), s32[32,3,1]{1,2,0:T(1,128)S(1)}, u32[]{:S(2)}, u32[]{:S(2)}) async-start(s32[32,3,1]{1,2,0:T(1,128)} %bitcast.8), calls=%async_computation | async-start | bytes 32768 | tf_op jit(solution)/shard_map/all_to_all | solution.py:112
  15.2 24.6 %copy-start.5 = (bf16[8,4096]{1,0:T(8,128)(2,1)S(1)}, bf16[8,4096]{1,0:T(8,128)(2,1)}, u32[]{:S(2)}) copy-start(bf16[8,4096]{1,0:T(8,128)(2,1)} %param.16) | copy-start | bytes 196612
  15.3 24.7 %copy-start.6 = (f32[4096]{0:T(1024)S(1)}, f32[4096]{0:T(1024)}, u32[]{:S(2)}) copy-start(f32[4096]{0:T(1024)} %param.28) | copy-start | bytes 49156
  25.2 13.0 %all-to-all-start.1 = ((bf16[32,3,512]{2,1,0:T(4,128)(2,1)}), bf16[32,3,512]{2,1,0:T(4,128)(2,1)S(1)}, u32[]{:S(2)}, u32[]{:S(2)}) async-start(bf16[32,3,512]{2,1,0:T(4,128)(2,1)} %all_to_all.30), calls=%async_computation.1 | async-start | bytes 262144 | tf_op jit(solution)/shard_map/all_to_all | solution.py:111
  205.5 8.1 %copy-start.2 = (bf16[640,4096]{1,0:T(8,128)(2,1)S(1)}, bf16[640,4096]{1,0:T(8,128)(2,1)}, u32[]{:S(2)}) copy-start(bf16[640,4096]{1,0:T(8,128)(2,1)} %all_to_all.34) | copy-start | bytes 15728644
  237.2 4.7 %copy-start.8 = (f32[64,8]{0,1:T(8,128)S(1)}, f32[64,8]{0,1:T(8,128)}, u32[]{:S(2)}) copy-start(f32[64,8]{0,1:T(8,128)} %param.27) | copy-start | bytes 6148
  237.2 140.8 %all-to-all-start.3 = ((bf16[32,20,4096]{2,1,0:T(8,128)(2,1)}), bf16[32,20,4096]{2,1,0:T(8,128)(2,1)}, u32[]{:S(2)}, u32[]{:S(2)}) async-start(bf16[32,20,4096]{2,1,0:T(8,128)(2,1)} %all_to_all.35), calls=%async_computation.3 | async-start | bytes 12582912 | tf_op jit(solution)/shard_map/all_to_all | solution.py:144
  385.8 17.4 %copy-start.1 = (bf16[64,16,512]{2,1,0:T(8,128)(2,1)S(1)}, bf16[64,16,512]{2,1,0:T(8,128)(2,1)}, u32[]{:S(2)}) copy-start(bf16[64,16,512]{2,1,0:T(8,128)(2,1)} %param.19) | copy-start | bytes 3145732
where the time goes:
time: 410 us; the launch traced here: 403 us
  waiting for transfers between devices  142 us (35%)
  blocking collectives  141 us (34%)
  local copies, waits for them, and re-layouts  61.8 us (15%)
  matrix products  28.9 us (7%)
  starting transfers between devices  16.6 us (4%)
  other arithmetic  11.6 us (3%)
    all_to_all x1, blocking collectives, on_device(): lax.all_to_all(outgoing, 'ep', split_axis=0, concat_axis=0, tiled=True)  141 us
    all_to_all x1, waiting for transfers between devices, on_device(): lax.all_to_all(summed, 'ep', split_axis=0, concat_axis=0, tiled=True)  136 us
    all_to_all x2, local copies, waits for them, and re-layouts, on_device(): lax.all_to_all(summed, 'ep', split_axis=0, concat_axis=0, tiled=True)  15.5 us
    gather x2, local copies, waits for them, and re-layouts, on_device(): normed[slot_source]  13.1 us
    gather x1, local copies, waits for them, and re-layouts, on_device(): picked = returned[slot_place].reshape(row_total, top_count, model_width)  11.8 us
    dot_general x1, matrix products, expert_terms(): return jnp.dot(hidden, down_weight[0], preferred_element_type=jnp.float32)  8.75 us
  transfers between devices with their start and end apart: 3, of which 2 were waited for; matrix products, arithmetic and copies ran while one was open for 4% of the time, Pallas kernels for 0%

commit v1 on v0

--- a/solution.py
+++ b/solution.py
@@ -1,6 +1,10 @@
+import functools
+
 import jax
 import jax.numpy as jnp
 from jax import lax
+from jax.experimental import pallas as pl
+from jax.experimental.pallas import tpu as pltpu
 from jax.sharding import PartitionSpec as P
 
 HD = 128
@@ -67,6 +71,334 @@
     up_act = jnp.dot(slot_rows, up_weight[0], preferred_element_type=jnp.float32)
     hidden = (jax.nn.silu(gate_act) * up_act).astype(jnp.bfloat16)
     return jnp.dot(hidden, down_weight[0], preferred_element_type=jnp.float32)
+
+
+def exchange_rows(residual_sum, normed, expert_ids, gate_values, gate_weight, up_weight, down_weight):
+    model_width = normed.shape[1]
+    row_total = normed.shape[0]
+    top_count = expert_ids.shape[1]
+    experts = lax.axis_size("ep")
+    capacity = min(
+        row_total, max(2, (5 * row_total * top_count + 4 * experts - 1) // (4 * experts))
+    )
+    chosen = expert_ids.reshape(-1)
+    chosen_hot = (chosen[:, None] == jnp.arange(experts, dtype=jnp.int32)[None, :]).astype(
+        jnp.int32
+    )
+    chosen_rank = jnp.sum(jnp.cumsum(chosen_hot, axis=0) * chosen_hot, axis=1) - 1
+    slot_place = chosen * capacity + chosen_rank
+    source_row = jnp.arange(row_total * top_count, dtype=jnp.int32) // top_count
+    slot_source = jnp.zeros((experts * capacity,), jnp.int32).at[slot_place].set(source_row)
+    slot_used = jnp.zeros((experts * capacity,), jnp.bool_).at[slot_place].set(True)
+    outgoing = jnp.where(slot_used[:, None], normed[slot_source], jnp.zeros((), jnp.bfloat16))
+    arrived = lax.all_to_all(outgoing, "ep", split_axis=0, concat_axis=0, tiled=True)
+    partial_out = expert_terms(
+        lax.all_gather(arrived, "ex", axis=0, tiled=True), gate_weight, up_weight, down_weight
+    )
+    summed = lax.psum_scatter(
+        partial_out.astype(jnp.bfloat16), "ex", scatter_dimension=0, tiled=True
+    )
+    returned = lax.all_to_all(summed, "ep", split_axis=0, concat_axis=0, tiled=True)
+    picked = returned[slot_place].reshape(row_total, top_count, model_width)
+    mixture = jnp.einsum("rk,rkd->rd", gate_values, picked.astype(jnp.float32))
+    return residual_sum + mixture
+
+
+def normalise(rows, norm_gain):
+    mean_square = jnp.mean(rows * rows, axis=1, keepdims=True)
+    return (rows * lax.rsqrt(mean_square + eps) * norm_gain).astype(jnp.bfloat16)
+
+
+def column_of(expert_ids, gate_values, experts):
+    numbers = jnp.arange(experts, dtype=jnp.int32)
+    return jnp.sum(
+        jnp.where(expert_ids[:, :, None] == numbers, gate_values[:, :, None], 0.0), axis=1
+    )
+
+
+def layer_kernel(
+    rows, normed, total, weight, gate_hbm, up_hbm, down_hbm, out,
+    held, gate, up, down, hidden, core_in, diag_in, side_in, far_in,
+    send_sem, recv_sem, load_sem,
+):
+    width = normed.shape[1]
+    half = width // 2
+    units = hidden.shape[1]
+    me = lax.axis_index("ep")
+    plane = me // 8
+    local = me % 8
+    sibling = me + 1 - 2 * (me % 2)
+    x_peer = me + 2 - 4 * ((me // 2) % 2)
+    y_peer = me + 4 - 8 * ((me // 4) % 2)
+    z_peer = (
+        me,
+        (plane + 1 - 2 * (plane % 2)) * 8 + local,
+        ((plane + 2) % 4) * 8 + local,
+        (3 - plane) * 8 + local,
+    )
+    loads = [
+        pltpu.make_async_copy(gate_hbm.at[0], gate, load_sem.at[0]),
+        pltpu.make_async_copy(up_hbm.at[0], up, load_sem.at[1]),
+        pltpu.make_async_copy(down_hbm.at[0], down, load_sem.at[2]),
+    ]
+    for load in loads:
+        load.start()
+    barrier = pltpu.get_barrier_semaphore()
+    for peer in (sibling, x_peer, y_peer) + z_peer[1:]:
+        pl.semaphore_signal(
+            barrier, inc=1, device_id={"ep": peer}, device_id_type=pl.DeviceIdType.MESH
+        )
+    pl.semaphore_wait(barrier, 6)
+
+    def remote(src, dst, k, slot, peer):
+        return pltpu.make_async_remote_copy(
+            src_ref=src,
+            dst_ref=dst,
+            send_sem=send_sem.at[k, slot],
+            recv_sem=recv_sem.at[k, slot],
+            device_id={"ep": peer},
+            device_id_type=pl.DeviceIdType.MESH,
+        )
+
+    def block(k, b):
+        return held.at[k, pl.ds(b * rows, rows), :]
+
+    def side(k, b, low):
+        return held.at[k, pl.ds(b * rows, rows), pl.ds(low, half)]
+
+    ag_z = [
+        remote(normed, block(k, 0), k, 0, z_peer[k]) if k else None for k in range(4)
+    ]
+    ag = []
+    rs = []
+    for k in range(4):
+        ag.append(
+            [
+                remote(block(k, 0), block(k, 1), k, 1, x_peer),
+                remote(block(k, 0), block(k, 2), k, 2, y_peer),
+                remote(side(k, 1, 0), side(k, 3, 0), k, 3, y_peer),
+                remote(side(k, 2, half), side(k, 3, half), k, 4, x_peer),
+                remote(block(k, 0), block(k, 4), k, 5, sibling),
+                remote(block(k, 1), block(k, 5), k, 6, sibling),
+                remote(block(k, 2), block(k, 6), k, 7, sibling),
+                remote(block(k, 3), block(k, 7), k, 8, sibling),
+            ]
+        )
+        rs.append(
+            [
+                remote(held.at[k, pl.ds(4 * rows, 4 * rows), :], core_in.at[k], k, 9, sibling),
+                remote(side(k, 3, 0), diag_in.at[k, 0], k, 10, y_peer),
+                remote(side(k, 3, half), diag_in.at[k, 1], k, 11, x_peer),
+                remote(block(k, 1), side_in.at[k, 0], k, 12, x_peer),
+                remote(block(k, 2), side_in.at[k, 1], k, 13, y_peer),
+                remote(block(k, 0), far_in.at[k - 1], k, 14, z_peer[k]) if k else None,
+            ]
+        )
+
+    def a1(k):
+        if k:
+            ag_z[k].wait_recv()
+        for i in (0, 1, 4):
+            ag[k][i].start()
+
+    def a2(k):
+        ag[k][0].wait_recv()
+        ag[k][2].start()
+        ag[k][5].start()
+        ag[k][1].wait_recv()
+        ag[k][3].start()
+        ag[k][6].start()
+
+    def a3(k):
+        ag[k][2].wait_recv()
+        ag[k][3].wait_recv()
+        ag[k][7].start()
+
+    def a4(k):
+        for i in range(4, 8):
+            ag[k][i].wait_recv()
+
+    def hidden_units(k):
+        tile = units // 3
+
+        @pl.loop(0, 3)
+        def _(n):
+            columns = pl.ds(pl.multiple_of(n * tile, tile), tile)
+            gate_act = jnp.dot(held[k], gate[:, columns], preferred_element_type=jnp.float32)
+            up_act = jnp.dot(held[k], up[:, columns], preferred_element_type=jnp.float32)
+            act = gate_act / (1.0 + jnp.exp(-gate_act)) * up_act
+            hidden[:, columns] = act.astype(jnp.bfloat16)
+
+    def down_units(k, part):
+        tile = 512
+        count = width // tile // 2
+
+        @pl.loop(part * count, (part + 1) * count)
+        def _(n):
+            columns = pl.ds(pl.multiple_of(n * tile, tile), tile)
+            term = jnp.dot(hidden[...], down[:, columns], preferred_element_type=jnp.float32)
+            held[k, :, columns] = (term * weight[k]).astype(jnp.bfloat16)
+
+    def add_into(k, b, low, size, source):
+        tile = 512
+
+        @pl.loop(0, size // tile)
+        def _(n):
+            mine = pl.ds(pl.multiple_of(low + n * tile, tile), tile)
+            theirs = pl.ds(pl.multiple_of(n * tile, tile), tile)
+            spot = pl.ds(b * rows, rows)
+            added = held[k, spot, mine].astype(jnp.float32)
+            for ref in source:
+                added = added + ref[:, theirs].astype(jnp.float32)
+            held[k, spot, mine] = added.astype(jnp.bfloat16)
+
+    def from_core(k, b):
+        return core_in.at[k, pl.ds(b * rows, rows), :]
+
+    def r1(k):
+        rs[k][0].start()
+
+    def r2(k):
+        rs[k][0].wait_recv()
+        add_into(k, 3, 0, width, [from_core(k, 3)])
+        rs[k][1].start()
+        rs[k][2].start()
+        add_into(k, 1, half, half, [core_in.at[k, pl.ds(rows, rows), pl.ds(half, half)]])
+        add_into(k, 2, 0, half, [core_in.at[k, pl.ds(2 * rows, rows), pl.ds(0, half)]])
+
+    def r3(k):
+        rs[k][1].wait_recv()
+        add_into(
+            k, 1, 0, half,
+            [core_in.at[k, pl.ds(rows, rows), pl.ds(0, half)], diag_in.at[k, 0]],
+        )
+        rs[k][3].start()
+        rs[k][2].wait_recv()
+        add_into(
+            k, 2, half, half,
+            [core_in.at[k, pl.ds(2 * rows, rows), pl.ds(half, half)], diag_in.at[k, 1]],
+        )
+        rs[k][4].start()
+
+    def r4(k):
+        rs[k][3].wait_recv()
+        rs[k][4].wait_recv()
+        add_into(k, 0, 0, width, [from_core(k, 0), side_in.at[k, 0], side_in.at[k, 1]])
+        if k:
+            rs[k][5].start()
+
+    def settle(k):
+        for copy in ag[k]:
+            copy.wait_send()
+
+    for k in (1, 2, 3):
+        ag_z[k].start()
+    held[0, pl.ds(0, rows), :] = normed[...]
+    a1(0)
+    a2(0)
+    a1(1)
+    a3(0)
+    a4(0)
+    a2(1)
+    loads[0].wait()
+    loads[1].wait()
+    loads[2].wait()
+    hidden_units(0)
+    settle(0)
+    a3(1)
+    a1(2)
+    down_units(0, 0)
+    a2(2)
+    down_units(0, 1)
+    r1(0)
+    a4(1)
+    a1(3)
+    hidden_units(1)
+    settle(1)
+    a3(2)
+    r2(0)
+    a2(3)
+    down_units(1, 0)
+    r3(0)
+    down_units(1, 1)
+    r1(1)
+    a4(2)
+    hidden_units(2)
+    settle(2)
+    a3(3)
+    r2(1)
+    down_units(2, 0)
+    r3(1)
+    down_units(2, 1)
+    r1(2)
+    a4(3)
+    r4(1)
+    hidden_units(3)
+    settle(3)
+    r2(2)
+    down_units(3, 0)
+    r3(2)
+    down_units(3, 1)
+    r1(3)
+    r4(2)
+    r4(0)
+    r2(3)
+    r3(3)
+    r4(3)
+    for k in (1, 2, 3):
+        rs[k][5].wait_recv()
+
+    @pl.loop(0, width // 512)
+    def _(n):
+        columns = pl.ds(pl.multiple_of(n * 512, 512), 512)
+        mixture = held[0, pl.ds(0, rows), columns].astype(jnp.float32)
+        for k in range(3):
+            mixture = mixture + far_in[k, :, columns].astype(jnp.float32)
+        out[:, columns] = (total[:, columns] + mixture).astype(jnp.bfloat16)
+
+    for k in range(4):
+        if k:
+            ag_z[k].wait_send()
+        for copy in rs[k]:
+            if copy is not None:
+                copy.wait_send()
+
+
+def fused_layer(residual_sum, normed, weight, gate_weight, up_weight, down_weight):
+    rows, width = normed.shape
+    units = gate_weight.shape[2]
+    bf16 = jnp.bfloat16
+    vmem = pl.BlockSpec(memory_space=pltpu.VMEM)
+    anywhere = pl.BlockSpec(memory_space=pl.ANY)
+    return pl.pallas_call(
+        functools.partial(layer_kernel, rows),
+        out_shape=jax.ShapeDtypeStruct((rows, width), bf16),
+        in_specs=[vmem] * 3 + [anywhere] * 3,
+        out_specs=vmem,
+        scratch_shapes=[
+            pltpu.VMEM((4, 8 * rows, width), bf16),
+            pltpu.VMEM((width, units), bf16),
+            pltpu.VMEM((width, units), bf16),
+            pltpu.VMEM((units, width), bf16),
+            pltpu.VMEM((8 * rows, units), bf16),
+            pltpu.VMEM((4, 4 * rows, width), bf16),
+            pltpu.VMEM((4, 2, rows, width // 2), bf16),
+            pltpu.VMEM((4, 2, rows, width), bf16),
+            pltpu.VMEM((3, rows, width), bf16),
+            pltpu.SemaphoreType.DMA((4, 15)),
+            pltpu.SemaphoreType.DMA((4, 15)),
+            pltpu.SemaphoreType.DMA((3,)),
+        ],
+        compiler_params=pltpu.CompilerParams(
+            collective_id=0, has_side_effects=True, vmem_limit_bytes=60 * 1024 * 1024
+        ),
+    )(normed, residual_sum, weight, gate_weight, up_weight, down_weight)
+
+
+def send_order():
+    block = jnp.arange(8, dtype=jnp.int32)
+    flips = (block % 2) * 2 + (block // 2 % 2) * 4 + block // 4
+    return (jnp.arange(4, dtype=jnp.int32)[:, None] * 8 + flips[None, :]).reshape(-1)
 
 
 def on_device(
@@ -88,7 +420,6 @@
     down_weight,
 ):
     decode_rows = residual.shape[0]
-    model_width = residual.shape[1]
     devices = lax.axis_size(("ep", "ex"))
     pre_rows = prefill_kv.shape[0]
     pages = page_table.reshape(decode_rows, -1)
@@ -107,44 +438,52 @@
         .set(prefill_kv)
     )
     send_slot = jnp.full((devices * kv_slots,), -1, jnp.int32).at[target_place].set(prefill_slot)
-    hand_kv, hand_slot = (
-        lax.all_to_all(send_kv, ("ep", "ex"), split_axis=0, concat_axis=0, tiled=True),
-        lax.all_to_all(send_slot, ("ep", "ex"), split_axis=0, concat_axis=0, tiled=True),
-    )
+    fused = lax.axis_size("ex") == 1 and devices == 32 and lax.axis_size("parts") == 1
+    if fused:
+        columns = column_of(expert_ids, gate_values, devices).T
+        high = lax.reduce_precision(columns, 8, 7)
+        low = columns - high
+        extra = jnp.concatenate(
+            [high, low, send_slot.reshape(devices, kv_slots).astype(jnp.float32)], axis=1
+        ).astype(jnp.bfloat16)
+        spare = prefill_kv.shape[1] - extra.shape[1]
+        payload = jnp.concatenate(
+            [
+                send_kv.reshape(devices, kv_slots, -1),
+                jnp.pad(extra, ((0, 0), (0, spare)))[:, None, :],
+            ],
+            axis=1,
+        )
+        payload = lax.all_to_all(payload, ("ep", "ex"), split_axis=0, concat_axis=0, tiled=True)
+        hand_kv = payload[:, :kv_slots].reshape(devices * kv_slots, -1)
+        extra = payload[:, kv_slots].astype(jnp.float32)
+        row_total = columns.shape[1]
+        weight = extra[:, :row_total] + extra[:, row_total : 2 * row_total]
+        hand_slot = extra[:, 2 * row_total : 2 * row_total + kv_slots].reshape(-1).astype(jnp.int32)
+    else:
+        hand_kv, hand_slot = (
+            lax.all_to_all(send_kv, ("ep", "ex"), split_axis=0, concat_axis=0, tiled=True),
+            lax.all_to_all(send_slot, ("ep", "ex"), split_axis=0, concat_axis=0, tiled=True),
+        )
     hand_ok = hand_slot[None, :] == jnp.arange(decode_rows, dtype=jnp.int32)[:, None]
     attention = attend(queries, new_kv, cache, lengths, hand_kv, hand_ok)
-    residual_sum = jnp.concatenate(
-        [residual.astype(jnp.float32) + attention, prefill_hidden.astype(jnp.float32)], axis=0
-    )
-    mean_square = jnp.mean(residual_sum * residual_sum, axis=1, keepdims=True)
-    normed = (residual_sum * lax.rsqrt(mean_square + eps) * norm_gain).astype(jnp.bfloat16)
-    row_total = normed.shape[0]
-    top_count = expert_ids.shape[1]
-    experts = lax.axis_size("ep")
-    capacity = min(
-        row_total, max(2, (5 * row_total * top_count + 4 * experts - 1) // (4 * experts))
-    )
-    chosen = expert_ids.reshape(-1)
-    chosen_hot = (chosen[:, None] == jnp.arange(experts, dtype=jnp.int32)[None, :]).astype(
-        jnp.int32
-    )
-    chosen_rank = jnp.sum(jnp.cumsum(chosen_hot, axis=0) * chosen_hot, axis=1) - 1
-    slot_place = chosen * capacity + chosen_rank
-    source_row = jnp.arange(row_total * top_count, dtype=jnp.int32) // top_count
-    slot_source = jnp.zeros((experts * capacity,), jnp.int32).at[slot_place].set(source_row)
-    slot_used = jnp.zeros((experts * capacity,), jnp.bool_).at[slot_place].set(True)
-    outgoing = jnp.where(slot_used[:, None], normed[slot_source], jnp.zeros((), jnp.bfloat16))
-    arrived = lax.all_to_all(outgoing, "ep", split_axis=0, concat_axis=0, tiled=True)
-    partial_out = expert_terms(
-        lax.all_gather(arrived, "ex", axis=0, tiled=True), gate_weight, up_weight, down_weight
-    )
-    summed = lax.psum_scatter(
-        partial_out.astype(jnp.bfloat16), "ex", scatter_dimension=0, tiled=True
-    )
-    returned = lax.all_to_all(summed, "ep", split_axis=0, concat_axis=0, tiled=True)
-    picked = returned[slot_place].reshape(row_total, top_count, model_width)
-    mixture = jnp.einsum("rk,rkd->rd", gate_values, picked.astype(jnp.float32))
-    result = (residual_sum + mixture).astype(jnp.bfloat16)
+    decode_sum = residual.astype(jnp.float32) + attention
+    prefill_sum = prefill_hidden.astype(jnp.float32)
+    weights = (gate_weight, up_weight, down_weight)
+    residual_sum = jnp.concatenate([decode_sum, prefill_sum], axis=0)
+    if fused:
+        normed = normalise(residual_sum, norm_gain)
+        order = lax.axis_index("ep") ^ send_order()
+        weight = weight[order].reshape(4, -1, 1)
+        result = fused_layer(residual_sum, normed, weight, *weights)
+        return (result[:decode_rows], result[decode_rows:])
+    result = exchange_rows(
+        residual_sum,
+        normalise(residual_sum, norm_gain),
+        expert_ids,
+        gate_values,
+        *weights,
+    ).astype(jnp.bfloat16)
     return (result[:decode_rows], result[decode_rows:])
 
 

time: 410 us -> 214 us (0.52); the launches traced: 403 us -> 213 us
  Pallas kernels: 0 us -> 181 us
  waiting for transfers between devices: 142 us -> 0.01 us
  blocking collectives: 141 us -> 0 us
  local copies, waits for them, and re-layouts: 61.8 us -> 12.3 us
  matrix products: 28.9 us -> 2.24 us
  starting transfers between devices: 16.6 us -> 6.1 us
    pallas_call x0 -> x1, Pallas kernels: none -> 181 us  [fused_layer(): pl.pallas_call(functools.partial(layer_kernel, rows), out_shape=jax.Shape...]
    all_to_all x3 -> x1, waiting for transfers between devices: 142 us -> 0.01 us  [on_device(): lax.all_to_all(payload, ('ep', 'ex'), split_axis=0, concat_axis=0, tiled=...]
    all_to_all x1 -> x0, blocking collectives: 141 us -> none  [on_device(): lax.all_to_all(outgoing, 'ep', split_axis=0, concat_axis=0, tiled=True)]
    dot_general x4 -> x0, matrix products: 27.4 us -> none  [the longest x1 8.75 us: expert_terms(): return jnp.dot(hidden, down_weight[0], preferred_element_type=jnp.float32)]
    all_to_all x7 -> x0, local copies, waits for them, and re-layouts: 25.4 us -> none  [the longest x2 15.5 us: on_device(): lax.all_to_all(summed, 'ep', split_axis=0, concat_axis=0, tiled=True)]
    gather x3 -> x1, local copies, waits for them, and re-layouts: 24.9 us -> 0.58 us  [on_device(): weight = weight[order].reshape(4, -1, 1)]
    all_to_all x3 -> x1, starting transfers between devices: 16.6 us -> 6.1 us  [on_device(): lax.all_to_all(payload, ('ep', 'ex'), split_axis=0, concat_axis=0, tiled=...]
    scatter x2 -> x0, local copies, waits for them, and re-layouts: 4.89 us -> none  [the longest x1 2.45 us: on_device(): jnp.zeros((experts * capacity,), jnp.bool_).at[slot_place].set(True)]
  transfers between devices with their start and end apart: 3 -> 1, of which waited for: 2 -> 0; matrix products, arithmetic and copies ran while one was open for 4% -> 3% of each run, Pallas kernels for 0% -> 0%
where the time goes in v1:
time: 214 us; the launch traced here: 213 us
  Pallas kernels  181 us (85%)
  local copies, waits for them, and re-layouts  12.3 us (6%)
  other arithmetic  10.8 us (5%)
  starting transfers between devices  6.1 us (3%)
  matrix products  2.24 us (1%)
    pallas_call x1, Pallas kernels, fused_layer(): pl.pallas_call(functools.partial(layer_kernel, rows), out_shape=jax.Shape...  181 us
    all_to_all x1, starting transfers between devices, on_device(): lax.all_to_all(payload, ('ep', 'ex'), split_axis=0, concat_axis=0, tiled=...  6.1 us
  transfers between devices with their start and end apart: 1, of which 0 were waited for; matrix products, arithmetic and copies ran while one was open for 3% of the time, Pallas kernels for 0%

profile of v1, /device:TPU:8, one launch (start us, length us, event | category | flops | bytes accessed | tf_op | source)
XLA Modules:
  0.0 213.2 jit_solution(1495382843627614426)
XLA Ops:
  0.6 0.0 copy-start
  0.6 0.0 copy-start.1
  0.7 0.8 fusion.25
  1.5 0.1 reduce_window_sum.11
  1.6 0.8 select_reduce_fusion.1
  2.4 0.7 fusion.36
  3.1 0.9 scatter_custom_fusion.1
  4.0 0.1 convert_element_type.62
  4.1 0.7 select_reduce_fusion
  4.8 0.1 fusion.23
  4.9 0.1 copy.132
  5.0 1.1 scatter_custom_fusion
  6.1 0.1 reshape.235
  6.2 0.8 pad_maximum_fusion.1
  7.0 0.0 copy-start.2
  7.0 6.1 %all-to-all-start = ((bf16[32,4,512]{2,1,0:T(4,128)(2,1)}), bf16[32,4,512]{2,1,0:T(4,128)(2,1)}, u32[]{:S(2)}, u32[]{:S(2)}) async-start(bf16[32,4,512]{2,1,0:T(4,128)(2,1)} %pad_maximum_fusion.1), calls=%async_computation | async-start | bytes 262144 | tf_op jit(solution)/shard_map/all_to_all | solution.py:457
  13.1 0.5 broadcast.266
  13.6 1.3 reduce.3
  14.9 0.1 reshape.231
  15.0 0.1 reshape.247
  15.1 0.0 copy-done
  15.1 0.6 gather_fusion
  15.7 0.1 fusion.41
  15.8 0.0 copy-start.3
  15.9 0.7 iota_compare_fusion.4
  16.6 0.7 bitcast_convert_fusion
  17.3 0.1 add_xor_fusion
  17.4 0.1 xor.18
  17.5 1.0 fusion.14
  18.5 0.3 copy.129
  18.7 0.3 copy.140
  19.0 1.1 convert_element_type.73
  20.1 0.0 copy-done.1
  20.1 0.3 fusion.43
  20.5 0.0 all-to-all-done
  20.5 1.0 slice.57
  21.5 0.1 slice_add_fusion
  21.6 1.0 reshape.236
  22.6 0.1 convert_element_type.66
  22.7 0.3 fusion.42
  23.0 0.2 fusion.6
  23.2 0.2 fusion.5
  23.5 0.3 convolution_bitcast_fusion
  23.7 0.4 fusion.2
  24.2 0.0 copy-done.2
  24.2 0.1 bitcast_add_fusion
  24.3 1.2 pad_maximum_fusion
  25.5 0.6 gather_fusion.1
  26.0 2.0 reshape.283.weight
  28.1 0.0 copy-done.3
  28.1 1.0 multiply_convert_fusion.normed
  29.1 180.8 %shard_map.167 = bf16[64,4096]{1,0:T(8,128)(2,1)} custom-call(bf16[64,4096]{1,0:T(8,128)(2,1)} %multiply_convert_fusion.normed, f32[64,4096]{1,0:T(8,128)} %get-tuple-element.4.total, f32[4,512,1]{2,1,0:T(8,128)} %reshape.283.weight, bf16[1,4096,768]{2,1,0:T(8,128)(2,1)} %gate_hbm.1, bf16[1,4096,768]{2,1,0:T(8,128)(2,1)} %up_hbm.1, ...), custom_call_target="tpu_custom_call" | custom-call | tf_op jit(solution)/shard_map/pallas_call | solution.py:373
  209.9 1.8 slice.51
  211.7 1.5 slice.50
  (20 shorter events, 0.1 us)
Async XLA Ops:
  0.6 14.5 %copy-start = (bf16[64,16,512]{2,1,0:T(8,128)(2,1)S(1)}, bf16[64,16,512]{2,1,0:T(8,128)(2,1)}, u32[]{:S(2)}) copy-start(bf16[64,16,512]{2,1,0:T(8,128)(2,1)} %param.19) | copy-start | bytes 3145732
  0.6 19.5 %copy-start.1 = (bf16[8,4096]{1,0:T(8,128)(2,1)S(1)}, bf16[8,4096]{1,0:T(8,128)(2,1)}, u32[]{:S(2)}) copy-start(bf16[8,4096]{1,0:T(8,128)(2,1)} %param.17) | copy-start | bytes 196612
  7.0 17.2 %copy-start.2 = (bf16[8,4096]{1,0:T(8,128)(2,1)S(1)}, bf16[8,4096]{1,0:T(8,128)(2,1)}, u32[]{:S(2)}) copy-start(bf16[8,4096]{1,0:T(8,128)(2,1)} %param.16) | copy-start | bytes 196612
  7.0 13.5 %all-to-all-start = ((bf16[32,4,512]{2,1,0:T(4,128)(2,1)}), bf16[32,4,512]{2,1,0:T(4,128)(2,1)}, u32[]{:S(2)}, u32[]{:S(2)}) async-start(bf16[32,4,512]{2,1,0:T(4,128)(2,1)} %pad_maximum_fusion.1), calls=%async_computation | async-start | bytes 262144 | tf_op jit(solution)/shard_map/all_to_all | solution.py:457
  15.8 12.2 %copy-start.3 = (f32[4096]{0:T(1024)S(1)}, f32[4096]{0:T(1024)}, u32[]{:S(2)}) copy-start(f32[4096]{0:T(1024)} %param.28) | copy-start | bytes 49156

commit v2 on v1

--- a/solution.py
+++ b/solution.py
@@ -218,16 +218,13 @@
         for i in range(4, 8):
             ag[k][i].wait_recv()
 
-    def hidden_units(k):
+    def hidden_units(k, n):
         tile = units // 3
-
-        @pl.loop(0, 3)
-        def _(n):
-            columns = pl.ds(pl.multiple_of(n * tile, tile), tile)
-            gate_act = jnp.dot(held[k], gate[:, columns], preferred_element_type=jnp.float32)
-            up_act = jnp.dot(held[k], up[:, columns], preferred_element_type=jnp.float32)
-            act = gate_act / (1.0 + jnp.exp(-gate_act)) * up_act
-            hidden[:, columns] = act.astype(jnp.bfloat16)
+        columns = pl.ds(n * tile, tile)
+        gate_act = jnp.dot(held[k], gate[:, columns], preferred_element_type=jnp.float32)
+        up_act = jnp.dot(held[k], up[:, columns], preferred_element_type=jnp.float32)
+        act = gate_act / (1.0 + jnp.exp(-gate_act)) * up_act
+        hidden[:, columns] = act.astype(jnp.bfloat16)
 
     def down_units(k, part):
         tile = 512
@@ -291,60 +288,81 @@
         for copy in ag[k]:
             copy.wait_send()
 
-    for k in (1, 2, 3):
-        ag_z[k].start()
+    inner = jnp.logical_or(plane == 1, plane == 2)
+    ag_z[1].start()
+
+    @pl.when(inner)
+    def _():
+        ag_z[3].start()
+
     held[0, pl.ds(0, rows), :] = normed[...]
     a1(0)
-    a2(0)
-    a1(1)
-    a3(0)
-    a4(0)
-    a2(1)
     loads[0].wait()
     loads[1].wait()
     loads[2].wait()
-    hidden_units(0)
+    ag_z[1].wait_send()
+    ag_z[2].start()
+    a1(1)
+    a2(0)
+    a3(0)
+    a4(0)
+    hidden_units(0, 0)
+    a2(1)
+    hidden_units(0, 1)
+    a3(1)
+    hidden_units(0, 2)
     settle(0)
-    a3(1)
+    ag_z[2].wait_send()
+
+    @pl.when(jnp.logical_not(inner))
+    def _():
+        ag_z[3].start()
+
     a1(2)
     down_units(0, 0)
-    a2(2)
     down_units(0, 1)
     r1(0)
     a4(1)
+    hidden_units(1, 0)
+    a2(2)
+    hidden_units(1, 1)
     a1(3)
-    hidden_units(1)
+    hidden_units(1, 2)
     settle(1)
     a3(2)
-    r2(0)
-    a2(3)
     down_units(1, 0)
-    r3(0)
     down_units(1, 1)
     r1(1)
+    r2(1)
+    a2(3)
     a4(2)
-    hidden_units(2)
+    hidden_units(2, 0)
+    r3(1)
+    hidden_units(2, 1)
+    a3(3)
+    hidden_units(2, 2)
     settle(2)
-    a3(3)
-    r2(1)
     down_units(2, 0)
-    r3(1)
     down_units(2, 1)
     r1(2)
+    r2(2)
+    r4(1)
     a4(3)
-    r4(1)
-    hidden_units(3)
+    hidden_units(3, 0)
+    r3(2)
+    hidden_units(3, 1)
+    hidden_units(3, 2)
     settle(3)
-    r2(2)
     down_units(3, 0)
-    r3(2)
     down_units(3, 1)
     r1(3)
+    r2(3)
     r4(2)
+    r2(0)
+    r3(3)
+    r3(0)
+    r4(3)
     r4(0)
-    r2(3)
-    r3(3)
-    r4(3)
     for k in (1, 2, 3):
         rs[k][5].wait_recv()
 
@@ -357,7 +375,7 @@
         out[:, columns] = (total[:, columns] + mixture).astype(jnp.bfloat16)
 
     for k in range(4):
-        if k:
+        if k == 3:
             ag_z[k].wait_send()
         for copy in rs[k]:
             if copy is not None:

time: 214 us -> 208 us (0.972)
  Pallas kernels: 181 us -> 174 us
    pallas_call x1, Pallas kernels: 181 us -> 174 us  [fused_layer(): pl.pallas_call(functools.partial(layer_kernel, rows), out_shape=jax.Shape...]
  transfers between devices with their start and end apart: 1 -> 1, of which waited for: 0 -> 0; matrix products, arithmetic and copies ran while one was open for 3% -> 4% of each run, Pallas kernels for 0% -> 0%
where the time goes in v2:
time: 208 us; the launch traced here: 206 us
  Pallas kernels  174 us (84%)
  local copies, waits for them, and re-layouts  12.3 us (6%)
  other arithmetic  10.8 us (5%)
  starting transfers between devices  6.1 us (3%)
  matrix products  2.24 us (1%)
    pallas_call x1, Pallas kernels, fused_layer(): pl.pallas_call(functools.partial(layer_kernel, rows), out_shape=jax.Shape...  174 us
    all_to_all x1, starting transfers between devices, on_device(): lax.all_to_all(payload, ('ep', 'ex'), split_axis=0, concat_axis=0, tiled=...  6.1 us
  transfers between devices with their start and end apart: 1, of which 0 were waited for; matrix products, arithmetic and copies ran while one was open for 4% of the time, Pallas kernels for 0%

profile of v2, /device:TPU:8, one launch (start us, length us, event | category | flops | bytes accessed | tf_op | source)
XLA Modules:
  0.0 206.1 jit_solution(11937315123389870438)
XLA Ops:
  0.6 0.0 copy-start
  0.6 0.0 copy-start.1
  0.7 0.8 fusion.25
  1.5 0.1 reduce_window_sum.11
  1.6 0.8 select_reduce_fusion.1
  2.4 0.7 fusion.36
  3.1 0.9 scatter_custom_fusion.1
  4.0 0.1 convert_element_type.62
  4.1 0.7 select_reduce_fusion
  4.8 0.1 fusion.23
  4.9 0.1 copy.132
  5.0 1.1 scatter_custom_fusion
  6.1 0.1 reshape.235
  6.2 0.8 pad_maximum_fusion.1
  7.0 0.0 copy-start.2
  7.0 6.1 %all-to-all-start = ((bf16[32,4,512]{2,1,0:T(4,128)(2,1)}), bf16[32,4,512]{2,1,0:T(4,128)(2,1)}, u32[]{:S(2)}, u32[]{:S(2)}) async-start(bf16[32,4,512]{2,1,0:T(4,128)(2,1)} %pad_maximum_fusion.1), calls=%async_computation | async-start | bytes 262144 | tf_op jit(solution)/shard_map/all_to_all | solution.py:475
  13.1 0.5 broadcast.266
  13.6 1.3 reduce.3
  14.9 0.1 reshape.231
  15.0 0.1 reshape.247
  15.1 0.0 copy-done
  15.1 0.6 gather_fusion
  15.7 0.1 fusion.41
  15.9 0.0 copy-start.3
  15.9 0.7 iota_compare_fusion.4
  16.6 0.7 bitcast_convert_fusion
  17.3 0.1 add_xor_fusion
  17.4 0.1 xor.18
  17.5 1.0 fusion.14
  18.5 0.3 copy.129
  18.8 0.3 copy.140
  19.0 1.1 convert_element_type.73
  20.1 0.0 copy-done.1
  20.1 0.3 fusion.43
  20.5 0.0 all-to-all-done
  20.5 1.0 slice.57
  21.5 0.1 slice_add_fusion
  21.6 1.0 reshape.236
  22.6 0.1 convert_element_type.66
  22.7 0.3 fusion.42
  23.0 0.2 fusion.6
  23.2 0.2 fusion.5
  23.5 0.3 convolution_bitcast_fusion
  23.7 0.4 fusion.2
  24.2 0.0 copy-done.2
  24.2 0.1 bitcast_add_fusion
  24.3 1.2 pad_maximum_fusion
  25.5 0.6 gather_fusion.1
  26.0 2.0 reshape.283.weight
  28.1 0.0 copy-done.3
  28.1 1.0 multiply_convert_fusion.normed
  29.1 173.8 %shard_map.167 = bf16[64,4096]{1,0:T(8,128)(2,1)} custom-call(bf16[64,4096]{1,0:T(8,128)(2,1)} %multiply_convert_fusion.normed, f32[64,4096]{1,0:T(8,128)} %get-tuple-element.4.total, f32[4,512,1]{2,1,0:T(8,128)} %reshape.283.weight, bf16[1,4096,768]{2,1,0:T(8,128)(2,1)} %gate_hbm.1, bf16[1,4096,768]{2,1,0:T(8,128)(2,1)} %up_hbm.1, ...), custom_call_target="tpu_custom_call" | custom-call | tf_op jit(solution)/shard_map/pallas_call | solution.py:391
  202.8 1.8 slice.51
  204.7 1.5 slice.50
  (20 shorter events, 0.1 us)
Async XLA Ops:
  0.6 14.5 %copy-start = (bf16[64,16,512]{2,1,0:T(8,128)(2,1)S(1)}, bf16[64,16,512]{2,1,0:T(8,128)(2,1)}, u32[]{:S(2)}) copy-start(bf16[64,16,512]{2,1,0:T(8,128)(2,1)} %param.19) | copy-start | bytes 3145732
  0.6 19.5 %copy-start.1 = (bf16[8,4096]{1,0:T(8,128)(2,1)S(1)}, bf16[8,4096]{1,0:T(8,128)(2,1)}, u32[]{:S(2)}) copy-start(bf16[8,4096]{1,0:T(8,128)(2,1)} %param.17) | copy-start | bytes 196612
  7.0 17.2 %copy-start.2 = (bf16[8,4096]{1,0:T(8,128)(2,1)S(1)}, bf16[8,4096]{1,0:T(8,128)(2,1)}, u32[]{:S(2)}) copy-start(bf16[8,4096]{1,0:T(8,128)(2,1)} %param.16) | copy-start | bytes 196612
  7.0 13.5 %all-to-all-start = ((bf16[32,4,512]{2,1,0:T(4,128)(2,1)}), bf16[32,4,512]{2,1,0:T(4,128)(2,1)}, u32[]{:S(2)}, u32[]{:S(2)}) async-start(bf16[32,4,512]{2,1,0:T(4,128)(2,1)} %pad_maximum_fusion.1), calls=%async_computation | async-start | bytes 262144 | tf_op jit(solution)/shard_map/all_to_all | solution.py:475
  15.9 12.2 %copy-start.3 = (f32[4096]{0:T(1024)S(1)}, f32[4096]{0:T(1024)}, u32[]{:S(2)}) copy-start(f32[4096]{0:T(1024)} %param.28) | copy-start | bytes 49156
